TPU v7x, 128 devices: a whole 4x4x4 slice. The times are simulated.
128 devices in a mesh: seq: 16 (over x, z), head: 8 (over y, core).
Axes of the slice: x: 4, y: 4, z: 4, core: 2. Of those that a mesh axis runs over, the one named last changes fastest.
Arguments:
- tokens: bfloat16 [8192, 8192], P('seq'), may hold values from -6 to 6
- w_query: bfloat16 [8192, 8192], P(None, 'head'), may hold values from -0.0625 to 0.0625
- w_key: bfloat16 [8192, 1024], P(None, 'head'), may hold values from -0.0625 to 0.0625
- w_value: bfloat16 [8192, 1024], P(None, 'head'), may hold values from -0.0625 to 0.0625
- b_query: bfloat16 [8192], P('head'), may hold values from -3 to 3
- b_key: bfloat16 [1024], P('head'), may hold values from -3 to 3
- b_value: bfloat16 [1024], P('head'), may hold values from -3 to 3
- prefix_keys: bfloat16 [16, 256, 1024], P('seq', None, 'head'), may hold values from -420 to 420
- prefix_values: bfloat16 [16, 256, 1024], P('seq', None, 'head'), may hold values from -6 to 6
- decode_rows: bfloat16 [64, 4, 8192], P('seq', None, 'head'), may hold values from -6 to 6
- page_table: int32 [64], replicated, may hold values from 0 to 63, as said below
- prompt_len: int32 [64], replicated, may hold values from 1 to 128
- soft_ids: int32 [64], replicated, may hold values from 0 to 15
- plan: int32 [128], replicated, may hold values from -1 to 63, as said below
Outputs:
- prefill_out: bfloat16 [8192, 8192], P('seq', 'head')
- decode_out: bfloat16 [128, 4, 8192], P('seq', None, 'head')
Inputs may be any that keep to these rules, and one draw needn't show every extreme that they name: `page_table`: the page of request r is one of pages 4 * (r // 4) to 4 * (r // 4) + 3; every page belongs to exactly one request. `plan`: every request stands in exactly one slot; no owner receives two requests of one block of 4 consecutive requests; some owner has all 8 slots used.
All inputs are finite; a program needn't handle non-finite values.
Results may differ from a plain program's by a relative error of at most 0.018.
Values may be sent and summed in bfloat16 or wider, within the bound.
A program may use at most 128 MiB of HBM per device.

v0:
```python
import math

import jax
import jax.numpy as jnp
from jax import lax
from jax.sharding import PartitionSpec as P

HD = 128


rope_theta = 1000000.0


def rotate(vectors, positions):
    half_dim = vectors.shape[-1] // 2
    frequency = rope_theta ** (-jnp.arange(half_dim, dtype=jnp.float32) * 2.0 / vectors.shape[-1])
    angles = positions.astype(jnp.float32)[..., None, None] * frequency
    cosine = jnp.cos(angles)
    sine_part = jnp.sin(angles)
    first_half = vectors[..., :half_dim]
    second = vectors[..., half_dim:]
    return jnp.concatenate(
        [first_half * cosine - second * sine_part, second * cosine + first_half * sine_part],
        axis=-1,
    )


def project(row_block, weight, bias_vec):
    return jnp.dot(row_block, weight, preferred_element_type=jnp.float32) + bias_vec.astype(
        jnp.float32
    )


def attend(queries, key_rows, value_rows, key_mask):
    inv_scale = 1.0 / math.sqrt(queries.shape[-1])
    scores = (
        jnp.einsum("brcgd,bscd->bcgrs", queries, key_rows, preferred_element_type=jnp.float32)
        * inv_scale
    )
    scores = jnp.where(key_mask[:, None, None], scores, -jnp.inf)
    row_max = jnp.max(scores, axis=-1, keepdims=True)
    exponent = jnp.exp(scores - row_max)
    weights = (exponent / jnp.sum(exponent, axis=-1, keepdims=True)).astype(jnp.bfloat16)
    return jnp.einsum("bcgrs,bscd->brcgd", weights, value_rows, preferred_element_type=jnp.float32)


def prefill(
    row_block,
    live_len,
    soft_pick,
    query_w,
    key_w,
    value_w,
    query_b,
    key_b,
    value_b,
    table_keys,
    table_values,
):
    page_count = live_len.shape[0]
    page_size = row_block.shape[0] // page_count
    kv_heads = key_w.shape[1] // HD
    groups = query_w.shape[1] // key_w.shape[1]
    offsets = jnp.arange(page_size, dtype=jnp.int32)
    live_mask = offsets[None, :] < live_len[:, None]
    positions = table_keys.shape[1] + jnp.broadcast_to(offsets[None, :], live_mask.shape)
    queries = rotate(
        project(row_block, query_w, query_b).reshape(page_count, page_size, kv_heads * groups, HD),
        positions,
    )
    queries = queries.astype(jnp.bfloat16).reshape(page_count, page_size, kv_heads, groups, HD)
    key_rows = rotate(
        project(row_block, key_w, key_b).reshape(page_count, page_size, kv_heads, HD), positions
    )
    key_rows = (key_rows * live_mask[:, :, None, None]).astype(jnp.bfloat16)
    value_rows = project(row_block, value_w, value_b).reshape(page_count, page_size, kv_heads, HD)
    value_rows = (value_rows * live_mask[:, :, None, None]).astype(jnp.bfloat16)
    prefix_size = table_keys.shape[1]
    fixed_keys = jnp.take(table_keys, soft_pick, axis=0).reshape(
        page_count, prefix_size, kv_heads, HD
    )
    fixed_values = jnp.take(table_values, soft_pick, axis=0).reshape(
        page_count, prefix_size, kv_heads, HD
    )
    causal = (offsets[None, :] <= offsets[:, None])[None] & live_mask[:, None, :]
    key_mask = jnp.concatenate(
        [jnp.ones((page_count, page_size, prefix_size), jnp.bool_), causal], axis=2
    )
    attended = attend(
        queries,
        jnp.concatenate([fixed_keys, key_rows], axis=1),
        jnp.concatenate([fixed_values, value_rows], axis=1),
        key_mask,
    )
    attended = (attended * live_mask[:, :, None, None, None]).astype(jnp.bfloat16)
    return (attended.reshape(page_count * page_size, kv_heads * groups * HD), key_rows, value_rows)


def decode(
    row_block,
    live_len,
    soft_pick,
    prompt_keys,
    prompt_values,
    query_w,
    key_w,
    value_w,
    query_b,
    key_b,
    value_b,
    table_keys,
    table_values,
):
    slot_count = row_block.shape[0]
    step_count = row_block.shape[1]
    kv_heads = key_w.shape[1] // HD
    groups = query_w.shape[1] // key_w.shape[1]
    flat_rows = row_block.reshape(slot_count * step_count, row_block.shape[2])
    prefix_size = table_keys.shape[1]
    step_ids = jnp.arange(step_count, dtype=jnp.int32)
    positions = prefix_size + live_len[:, None] + step_ids[None, :]
    queries = rotate(
        project(flat_rows, query_w, query_b).reshape(slot_count, step_count, kv_heads * groups, HD),
        positions,
    )
    queries = queries.astype(jnp.bfloat16).reshape(slot_count, step_count, kv_heads, groups, HD)
    key_rows = rotate(
        project(flat_rows, key_w, key_b).reshape(slot_count, step_count, kv_heads, HD), positions
    ).astype(jnp.bfloat16)
    value_rows = (
        project(flat_rows, value_w, value_b)
        .reshape(slot_count, step_count, kv_heads, HD)
        .astype(jnp.bfloat16)
    )
    page_size = prompt_keys.shape[1]
    fixed_keys = jnp.take(table_keys, soft_pick, axis=0).reshape(
        slot_count, prefix_size, kv_heads, HD
    )
    fixed_values = jnp.take(table_values, soft_pick, axis=0).reshape(
        slot_count, prefix_size, kv_heads, HD
    )
    prompt_live = jnp.arange(page_size, dtype=jnp.int32)[None, :] < live_len[:, None]
    causal = step_ids[None, :] <= step_ids[:, None]
    key_mask = jnp.concatenate(
        [
            jnp.ones((slot_count, step_count, prefix_size), jnp.bool_),
            jnp.broadcast_to(prompt_live[:, None, :], (slot_count, step_count, page_size)),
            jnp.broadcast_to(causal[None], (slot_count, step_count, step_count)),
        ],
        axis=2,
    )
    all_keys = jnp.concatenate([fixed_keys, prompt_keys, key_rows], axis=1)
    all_values = jnp.concatenate([fixed_values, prompt_values, value_rows], axis=1)
    return attend(queries, all_keys, all_values, key_mask)


def body(
    tokens,
    w_query,
    w_key,
    w_value,
    b_query,
    b_key,
    b_value,
    prefix_keys,
    prefix_values,
    decode_rows,
    page_table,
    prompt_len,
    soft_ids,
    plan,
):
    senders = lax.axis_size("seq")
    seq_index = lax.axis_index("seq")
    req_dev = decode_rows.shape[0]
    capacity = plan.shape[0] // senders
    table_keys, table_values = (
        lax.all_gather(prefix_keys, "seq", axis=0, tiled=True),
        lax.all_gather(prefix_values, "seq", axis=0, tiled=True),
    )
    block_start = seq_index * req_dev
    local_ids = block_start + jnp.arange(req_dev, dtype=jnp.int32)
    everyone = jnp.arange(page_table.shape[0], dtype=jnp.int32)
    holder = jnp.sum(
        jnp.where(page_table[None, :] == local_ids[:, None], everyone[None, :], 0), axis=1
    )
    prefill_out, key_rows, value_rows = prefill(
        tokens,
        prompt_len[holder],
        soft_ids[holder],
        w_query,
        w_key,
        w_value,
        b_query,
        b_key,
        b_value,
        table_keys,
        table_values,
    )
    own_page = lax.dynamic_slice_in_dim(page_table, block_start, req_dev) - block_start
    page_size = key_rows.shape[1]
    row_width = key_rows.shape[2] * key_rows.shape[3]
    sent_keys = jnp.take(key_rows, own_page, axis=0).reshape(req_dev, page_size, row_width)
    sent_values = jnp.take(value_rows, own_page, axis=0).reshape(req_dev, page_size, row_width)
    slot_req = lax.dynamic_slice_in_dim(plan, seq_index * capacity, capacity)
    live_slot = slot_req >= 0
    wanted = jnp.maximum(slot_req, 0)
    initial = (
        jnp.zeros((capacity,) + sent_keys.shape[1:], sent_keys.dtype),
        jnp.zeros((capacity,) + sent_values.shape[1:], sent_values.dtype),
        jnp.zeros((capacity,) + decode_rows.shape[1:], decode_rows.dtype),
    )
    portion = (
        lax.all_gather(sent_keys, "seq", axis=0, tiled=True),
        lax.all_gather(sent_values, "seq", axis=0, tiled=True),
        lax.all_gather(decode_rows, "seq", axis=0, tiled=True),
    )
    portion_len = portion[0].shape[0]
    inside = live_slot & (wanted >= 0) & (wanted < portion_len)
    clipped = jnp.clip(wanted, 0, portion_len - 1)
    own_keys, own_values, own_rows = tuple(
        (
            jnp.where(
                inside.reshape((-1,) + (1,) * (member.ndim - 1)),
                jnp.take(member, clipped, axis=0),
                held,
            )
            for held, member in zip(initial, portion)
        )
    )
    full_rows = lax.all_gather(own_rows, "head", axis=2, tiled=True)
    decoded = decode(
        full_rows,
        prompt_len[wanted],
        soft_ids[wanted],
        own_keys.reshape(capacity, page_size, -1, HD),
        own_values.reshape(capacity, page_size, -1, HD),
        w_query,
        w_key,
        w_value,
        b_query,
        b_key,
        b_value,
        table_keys,
        table_values,
    )
    decode_out = (
        (decoded * live_slot[:, None, None, None, None])
        .astype(jnp.bfloat16)
        .reshape(capacity, full_rows.shape[1], -1)
    )
    return (prefill_out, decode_out)


def solution(mesh):
    in_specs = (
        P("seq", None),
        P(None, "head"),
        P(None, "head"),
        P(None, "head"),
        P("head"),
        P("head"),
        P("head"),
        P("seq", None, "head"),
        P("seq", None, "head"),
        P("seq", None, "head"),
        P(),
        P(),
        P(),
        P(),
    )
    out_specs = (P("seq", "head"), P("seq", None, "head"))
    return jax.shard_map(body, mesh=mesh, in_specs=in_specs, out_specs=out_specs, check_vma=False)
```

profile of v0, /device:TPU:0, one launch (start us, length us, event | category | flops | bytes accessed | tf_op | source)
XLA Modules:
  0.0 204.6 jit_solution(12948457596032918659)
XLA Ops:
  11.7 1.3 gather_fusion.1
  13.1 6.0 %convolution_add_fusion = f32[512,128]{1,0:T(8,128)S(1)} fusion(bf16[512,8192]{1,0:T(8,128)(2,1)} %param.22, bf16[8192,128]{1,0:T(8,128)(2,1)S(1)} %copy-done, f32[128]{0:T(128)S(1)} %convert_element_type.130), kind=kOutput, calls=%fused_computation.30 | convolution fusion | flops 1073807360 | bytes 10748416 | tf_op jit(solution)/shard_map/dot_general | solution.py:29
  19.6 2.4 %convolution_add_fusion.1 = f32[512,128]{1,0:T(8,128)S(1)} fusion(bf16[512,8192]{1,0:T(8,128)(2,1)S(1)} %copy-done.30, bf16[8192,128]{1,0:T(8,128)(2,1)S(1)} %copy-done.3, f32[128]{0:T(128)S(1)} %convert_element_type.127), kind=kOutput, calls=%fused_computation.31 | convolution fusion | flops 1073807360 | bytes 10748416 | tf_op jit(solution)/shard_map/dot_general | solution.py:29
  31.2 26.2 %all_gather.21 = bf16[64,4,1024]{2,1,0:T(4,128)(2,1)S(1)} all-gather(bf16[4,4,1024]{2,1,0:T(4,128)(2,1)S(1)} %copy-done.11), channel_id=1, replica_groups=mesh['seq'=16,'head'=8] {'seq'}, dimensions={0}, use_global_device_ids=true | all-gather | bytes 557056 | tf_op jit(solution)/shard_map/all_gather | solution.py:216
  58.1 13.5 %all_gather.22 = bf16[8,4,8192]{2,1,0:T(4,128)(2,1)S(1)} all-gather(bf16[8,4,1024]{2,1,0:T(4,128)(2,1)S(1)} %select_select_fusion.2), channel_id=1, replica_groups=mesh['seq'=16,'head'=8] {'head'}, dimensions={2}, use_global_device_ids=true | all-gather | bytes 589824 | tf_op jit(solution)/shard_map/all_gather | solution.py:231
  72.3 9.0 %fusion.14 = f32[4,8,8,128]{3,1,2,0:T(8,128)S(1)} fusion(bf16[32,8192]{1,0:T(8,128)(2,1)S(1)} %reshape.450, bf16[8192,1024]{1,0:T(8,128)(2,1)} %param.23, f32[1024]{0:T(1024)S(1)} %convert_element_type.133), kind=kOutput, calls=%fused_computation.35 | convolution fusion | flops 536903680 | bytes 17436672 | tf_op jit(solution)/shard_map/dot_general | solution.py:29
  81.3 13.7 %add_bitcast_fusion = f32[64,8,8,128]{3,1,2,0:T(8,128)} fusion(bf16[512,8192]{1,0:T(8,128)(2,1)S(1)} %bitcast.158, bf16[8192,1024]{1,0:T(8,128)(2,1)} %param.23, f32[1024]{0:T(1024)S(1)} %convert_element_type.133), kind=kOutput, calls=%fused_computation.25 | convolution fusion | flops 8590458880 | bytes 27267072 | tf_op jit(solution)/shard_map/dot_general | solution.py:29
  98.5 2.2 %copy.49 = f32[64,8,8,128]{3,2,1,0:T(8,128)S(1)} copy(f32[64,8,8,128]{3,1,2,0:T(8,128)} %add_bitcast_fusion) | data formatting | bytes 4194304
  103.4 1.8 subtract_convert_fusion
  105.3 2.6 %gather_fusion.5 = bf16[4,256,128]{2,1,0:T(8,128)(2,1)} fusion(bf16[16,256,128]{2,1,0:T(8,128)(2,1)} %all-gather.7.cloned.1.call-done, s32[1024]{0:T(1024)} %pad_clamp_fusion.4), kind=kCustom, calls=%fused_computation.clone | custom fusion | bytes 524304 | tf_op jit(solution)/shard_map/jit(_take)/gather | solution.py:82
  107.9 1.8 copy.34
  109.7 2.6 %gather_fusion.6 = bf16[4,256,128]{2,1,0:T(8,128)(2,1)} fusion(bf16[16,256,128]{2,1,0:T(8,128)(2,1)} %all-gather.9.cloned.1.call-done, s32[1024]{0:T(1024)} %pad_clamp_fusion.4), kind=kCustom, calls=%fused_computation.4.clone | custom fusion | bytes 524304 | tf_op jit(solution)/shard_map/jit(_take)/gather | solution.py:79
  114.4 2.8 %fusion.1 = (f32[4,8,128]{2,1,0:T(8,128)S(1)}, f32[4,384,128,8]{2,1,3,0:T(8,128)S(1)}) fusion(pred[4,128,384]{1,2,0:T(8,128)(4,1)S(1)} %concatenate.54, bf16[4,128,8,64]{3,1,2,0:T(8,128)(2,1)} %get-tuple-element.13, bf16[4,128,8,64]{3,1,2,0:T(8,128)(2,1)S(1)} %get-tuple-element.12, bf16[4,128,1,128]{3,1,0,2:T(8,128)(2,1)S(1)} %get-tuple-element.25, ...), kind=kOutput, calls=%fused_computation.17 | convolution fusion | flops 410251264 | bytes 7946240 | tf_op jit(solution)/shard_map/brcgd,bscd->bcgrs/dot_general | solution.py:37
  117.2 1.4 fusion
  118.7 2.9 %fusion.8 = bf16[4,128,1,8,128]{1,4,3,0,2:T(8,128)(2,1)} fusion(f32[4,8,128]{2,1,0:T(8,128)S(1)} %fusion, f32[4,8,128]{2,1,0:T(8,128)S(1)} %get-tuple-element.37, f32[4,384,128,8]{2,1,3,0:T(8,128)S(1)} %get-tuple-element.38, pred[4,128,384]{1,2,0:T(8,128)(4,1)S(1)} %concatenate.54, f32[4,128]{1,0:T(4,128)S(1)} %copy-done.14, ...), kind=kOutput, calls=%fused_computation.26 | convolution fusion | flops 412352512 | bytes 7964672 | tf_op jit(solution)/shard_map/bcgrs,bscd->brcgd/dot_general | solution.py:44
  121.6 1.7 copy.39
  123.3 1.2 copy.57
  124.6 2.0 gather_fusion.10
  126.6 2.0 gather_fusion.7
  128.6 1.2 select_bitcast_fusion
  129.8 17.2 %all-gather.13.cloned.1.call-done = bf16[64,128,1,128]{3,1,2,0:T(8,128)(2,1)} async-done(((bf16[4,128,1,128]{3,1,2,0:T(8,128)(2,1)}), bf16[64,128,1,128]{3,1,2,0:T(8,128)(2,1)}) %all-gather.13.cloned.1.call-update) | async-done | bytes 2097168 | tf_op jit(solution)/shard_map/all_gather | solution.py:214
  147.0 2.3 %gather_fusion.12 = bf16[8,128,128]{2,1,0:T(8,128)(2,1)S(1)} fusion(bf16[64,128,128]{2,1,0:T(8,128)(2,1)} %bitcast.154, s32[1024]{0:T(1024)} %copy-done.17), kind=kCustom, calls=%fused_computation.7.clone | custom fusion | bytes 524320 | tf_op jit(solution)/shard_map/jit(_take)/gather | solution.py:225
  149.3 44.2 %all-gather.11.cloned.1.call-done = bf16[64,128,1,128]{3,1,2,0:T(8,128)(2,1)} async-done(((bf16[4,128,1,128]{3,1,2,0:T(8,128)(2,1)}), bf16[64,128,1,128]{3,1,2,0:T(8,128)(2,1)}) %all-gather.11.cloned.1.call-update) | async-done | bytes 2097168 | tf_op jit(solution)/shard_map/all_gather | solution.py:215
  193.5 2.3 %gather_fusion.9 = bf16[8,128,128]{2,1,0:T(8,128)(2,1)S(1)} fusion(bf16[64,128,128]{2,1,0:T(8,128)(2,1)} %bitcast.155, s32[1024]{0:T(1024)} %copy-done.17), kind=kCustom, calls=%fused_computation.3.clone | custom fusion | bytes 524320 | tf_op jit(solution)/shard_map/jit(_take)/gather | solution.py:225
  (139 shorter events, 25.6 us)
Async XLA Ops:
  7.2 5.9 %copy-start = (bf16[8192,128]{1,0:T(8,128)(2,1)S(1)}, bf16[8192,128]{1,0:T(8,128)(2,1)}, u32[]{:S(2)}) copy-start(bf16[8192,128]{1,0:T(8,128)(2,1)} %param.24) | copy-start | bytes 6291460
  7.2 98.1 %all-gather.7.cloned.1.call-start = ((), (), s32[]{:S(2)}) async-start(), calls=%async_computation | async-start | bytes 1114112 | tf_op jit(solution)/shard_map/all_gather | solution.py:179
  7.9 101.8 %all-gather.9.cloned.1.call-start = ((), (), s32[]{:S(2)}) async-start(), calls=%async_computation.1 | async-start | bytes 1114112 | tf_op jit(solution)/shard_map/all_gather | solution.py:178
  8.7 138.3 %all-gather.13.cloned.1.call-start = ((), (), s32[]{:S(2)}) async-start(), calls=%async_computation.3 | async-start | bytes 2228224 | tf_op jit(solution)/shard_map/all_gather | solution.py:214
  10.1 9.5 %copy-start.28 = (f32[128]{0:T(128)}, f32[128]{0:T(128)S(1)}, u32[]{:S(2)}) copy-start(f32[128]{0:T(128)S(1)} %convert_element_type.127) | copy-start | bytes 1540
  13.0 9.0 %copy-start.13 = (f32[4,128]{1,0:T(4,128)}, f32[4,128]{1,0:T(4,128)S(1)}, u32[]{:S(2)}) copy-start(f32[4,128]{1,0:T(4,128)S(1)} %get-tuple-element.36) | copy-start | bytes 6148
  13.1 6.5 %copy-start.3 = (bf16[8192,128]{1,0:T(8,128)(2,1)S(1)}, bf16[8192,128]{1,0:T(8,128)(2,1)}, u32[]{:S(2)}) copy-start(bf16[8192,128]{1,0:T(8,128)(2,1)} %param.25) | copy-start | bytes 6291460
  13.1 6.5 %copy-start.30 = (bf16[512,8192]{1,0:T(8,128)(2,1)S(1)}, bf16[512,8192]{1,0:T(8,128)(2,1)}, u32[]{:S(2)}) copy-start(bf16[512,8192]{1,0:T(8,128)(2,1)} %param.22) | copy-start | bytes 25165828
  22.1 9.0 %copy-start.22 = (bf16[1024]{0:T(1024)(128)(2,1)S(1)}, bf16[1024]{0:T(1024)(128)(2,1)}, u32[]{:S(2)}) copy-start(bf16[1024]{0:T(1024)(128)(2,1)} %param.26) | copy-start | bytes 6148
  22.1 9.1 %copy-start.11 = (bf16[4,4,1024]{2,1,0:T(4,128)(2,1)S(1)}, bf16[4,4,1024]{2,1,0:T(4,128)(2,1)}, u32[]{:S(2)}) copy-start(bf16[4,4,1024]{2,1,0:T(4,128)(2,1)} %param.31) | copy-start | bytes 98308
  24.3 169.2 %all-gather.11.cloned.1.call-start = ((), (), s32[]{:S(2)}) async-start(), calls=%async_computation.2 | async-start | bytes 2228224 | tf_op jit(solution)/shard_map/all_gather | solution.py:215
  25.5 32.4 %copy-start.18 = (pred[8]{0:T(512)(128)(4,1)}, pred[8]{0:T(512)(128)(4,1)S(1)}, u32[]{:S(2)}) copy-start(pred[8]{0:T(512)(128)(4,1)S(1)} %get-tuple-element.10) | copy-start | bytes 28
  25.6 32.4 %copy-start.20 = (pred[8]{0:T(512)(128)(4,1)}, pred[8]{0:T(512)(128)(4,1)S(1)}, u32[]{:S(2)}) copy-start(pred[8]{0:T(512)(128)(4,1)S(1)} %get-tuple-element.34) | copy-start | bytes 28
  31.1 26.8 %copy-start.17 = (s32[1024]{0:T(1024)}, s32[1024]{0:T(1024)S(1)}, u32[]{:S(2)}) copy-start(s32[1024]{0:T(1024)S(1)} %pad_clamp_fusion) | copy-start | bytes 12292
  71.8 9.5 %slice-start = ((s8[8388608]{0:T(1024)(128)(4,1)}), s8[4194304]{0:T(1024)(128)(4,1)S(1)}, s32[]{:S(2)}) async-start(s8[8388608]{0:T(1024)(128)(4,1)} %bitcast.157), calls=%async_computation.4 | async-start | bytes 8388608
  72.2 9.1 %slice-start.1 = ((s8[8388608]{0:T(1024)(128)(4,1)}), s8[4194304]{0:T(1024)(128)(4,1)S(1)}, s32[]{:S(2)}) async-start(s8[8388608]{0:T(1024)(128)(4,1)} %bitcast.157), calls=%async_computation.5 | async-start | bytes 8388608
  81.3 15.8 %copy-start.25 = (s32[8]{0:T(128)S(1)}, s32[8]{0:T(128)}, u32[]{:S(2)}) copy-start(s32[8]{0:T(128)} %compare_select_fusion.2) | copy-start | bytes 100
  123.3 5.3 %copy-start.23 = (pred[8]{0:T(512)(128)(4,1)S(1)}, pred[8]{0:T(512)(128)(4,1)}, u32[]{:S(2)}) copy-start(pred[8]{0:T(512)(128)(4,1)} %compare_and_fusion.2) | copy-start | bytes 28
  126.6 69.3 %copy-start.19 = (pred[8]{0:T(512)(128)(4,1)S(1)}, pred[8]{0:T(512)(128)(4,1)}, u32[]{:S(2)}) copy-start(pred[8]{0:T(512)(128)(4,1)} %copy-done.18) | copy-start | bytes 28
  126.6 69.3 %copy-start.21 = (pred[8]{0:T(512)(128)(4,1)S(1)}, pred[8]{0:T(512)(128)(4,1)}, u32[]{:S(2)}) copy-start(pred[8]{0:T(512)(128)(4,1)} %copy-done.20) | copy-start | bytes 28
  128.6 67.4 %copy-start.10 = (bf16[8,4,8,64]{3,2,1,0:T(8,128)(2,1)S(1)}, bf16[8,4,8,64]{3,2,1,0:T(8,128)(2,1)}, u32[]{:S(2)}) copy-start(bf16[8,4,8,64]{3,2,1,0:T(8,128)(2,1)} %get-tuple-element.19) | copy-start | bytes 98308
  128.6 67.4 %copy-start.15 = (bf16[8,4,1,64]{3,1,0,2:T(4,128)(2,1)S(1)}, bf16[8,4,1,64]{3,1,0,2:T(4,128)(2,1)}, u32[]{:S(2)}) copy-start(bf16[8,4,1,64]{3,1,0,2:T(4,128)(2,1)} %get-tuple-element.20) | copy-start | bytes 12292
  128.6 67.4 %copy-start.16 = (bf16[8,4,1,64]{3,1,0,2:T(4,128)(2,1)S(1)}, bf16[8,4,1,64]{3,1,0,2:T(4,128)(2,1)}, u32[]{:S(2)}) copy-start(bf16[8,4,1,64]{3,1,0,2:T(4,128)(2,1)} %get-tuple-element.21) | copy-start | bytes 12292
  129.8 66.3 %copy-start.8 = (bf16[8,256,1,128]{3,1,0,2:T(8,128)(2,1)S(1)}, bf16[8,256,1,128]{3,1,0,2:T(8,128)(2,1)}, u32[]{:S(2)}) copy-start(bf16[8,256,1,128]{3,1,0,2:T(8,128)(2,1)} %get-tuple-element.30) | copy-start | bytes 1572868
  (13 other events, 26.5 us)
Sparse Core Ops, SparseCore 0:
  10.2 45.7 all-gather.6
  58.1 42.1 all-gather.8
  102.4 44.5 all-gather.12
  149.0 44.5 all-gather.10
where the time goes:
time: 205 us
  waiting for transfers between devices  63.3 us (31%)
  blocking collectives  39.7 us (19%)
  matrix products  39.3 us (19%)
  local copies, waits for them, and re-layouts  28.7 us (14%)
  other arithmetic  18.9 us (9%)
  between operations  14.5 us (7%)
    all_gather x1, waiting for transfers between devices, body(): lax.all_gather(sent_values, 'seq', axis=0, tiled=True)  44.2 us
    dot_general x6, matrix products, project(): jnp.dot(row_block, weight, preferred_element_type=jnp.float32)  32.7 us
    all_gather x1, blocking collectives, body(): lax.all_gather(decode_rows, 'seq', axis=0, tiled=True)  26.2 us
    all_gather x1, waiting for transfers between devices, body(): lax.all_gather(sent_keys, 'seq', axis=0, tiled=True)  17.2 us
    all_gather x1, blocking collectives, body(): full_rows = lax.all_gather(own_rows, 'head', axis=2, tiled=True)  13.5 us
    gather x3, local copies, waits for them, and re-layouts, body(): jnp.take(member, clipped, axis=0)  5.22 us
    gather x2, local copies, waits for them, and re-layouts, prefill(): jnp.take(table_values, soft_pick, axis=0)  4.42 us
    unnamed x69, local copies, waits for them, and re-layouts  4.14 us
  transfers between devices with their start and end apart: 4, of which 2 were waited for; matrix products, arithmetic and copies ran while one was open for 40% of the time, Pallas kernels for 0%

commit v1 on v0

v1 whole, which is shorter than its diff:
```python
import functools
import math

import jax
import jax.numpy as jnp
import numpy as np
from jax import lax
from jax.experimental import pallas as pl
from jax.experimental.pallas import tpu as pltpu
from jax.sharding import PartitionSpec as P

HD = 128
PAGE = 128
PFX = 256
STEPS = 4
REQ = 4
SLOTS = 8
NS = 16
NH = 8
GROUP = 8
D = 8192
TOK = REQ * PAGE
ROWS = TOK + REQ * STEPS
QW = GROUP * HD
W = QW + 2 * HD
KC = 512
NC = D // KC
PER = NC // NH
LOOK = 4
PIECE = PFX // NS
HEADS_AT_ONCE = 2
MESH = pl.DeviceIdType.MESH
EXP2_SCALE = math.log2(math.e) / math.sqrt(HD)
ROPE_ROWS = 136


def rope_table():
    frequency = 1000000.0 ** (-np.arange(HD // 2, dtype=np.float64) * 2.0 / HD)
    angles = (PFX + np.arange(ROPE_ROWS, dtype=np.float64))[:, None] * frequency
    cosine = np.concatenate([np.cos(angles), np.cos(angles)], axis=1)
    sine = np.concatenate([-np.sin(angles), np.sin(angles)], axis=1)
    return np.stack([cosine, sine]).astype(np.float32)


def rotate(vectors, cosine, sine):
    return vectors * cosine + pltpu.roll(vectors, HD // 2, 1) * sine


def scores_of(queries, keys):
    return lax.dot_general(queries, keys, (((1,), (1,)), ((), ())), preferred_element_type=jnp.float32)


def kernel(
    tokens, w_query, w_key, w_value, b_query, b_key, b_value, prefix_keys, prefix_values, decode_rows,
    page_table, prompt_len, soft_ids, plan, rope,
    prefill_out, decode_out,
    x, w, acc, queries, keys, values, key_all, value_all, out_stage,
    bq, bk, bv, rope_v, drows, drow_stage, piece, dealt, picked, prefix, dq, dk, dv, dec_keys, dec_values, dec_f32,
    dec_res, dec_send, dec_recv, dec_out_v,
    table_s, len_s, soft_s, plan_s,
    chunk_sem, small_sem, out_sem, rows_send, rows_recv, deal_send, deal_recv, pick_send, pick_recv, res_send, res_recv,
):
    s = lax.axis_index("seq")
    h = lax.axis_index("head")

    def chunk_copies(i):
        c = lax.rem(PER * h + i, NC)
        at = pl.ds(pl.multiple_of(c * KC, KC), KC)
        return (
            pltpu.make_async_copy(tokens.at[:, at], x.at[c, pl.ds(0, TOK), :], chunk_sem.at[0, c]),
            pltpu.make_async_copy(w_query.at[at, :], w.at[c, :, pl.ds(0, QW)], chunk_sem.at[1, c]),
            pltpu.make_async_copy(w_key.at[at, :], w.at[c, :, pl.ds(QW, HD)], chunk_sem.at[2, c]),
            pltpu.make_async_copy(w_value.at[at, :], w.at[c, :, pl.ds(QW + HD, HD)], chunk_sem.at[3, c]),
        )

    small = [
        pltpu.make_async_copy(src, dst, small_sem.at[n])
        for n, (src, dst) in enumerate(
            (
                (prefix_keys, piece.at[:, pl.ds(0, PIECE), :]),
                (prefix_values, piece.at[:, pl.ds(PIECE, PIECE), :]),
                (decode_rows, drows),
                (page_table, table_s),
                (prompt_len, len_s),
                (soft_ids, soft_s),
                (plan, plan_s),
                (b_query, bq),
                (b_key, bk),
                (b_value, bv),
                (rope, rope_v),
            )
        )
    ]

    barrier = pltpu.get_barrier_semaphore()

    def greet_seq(k, _):
        pl.semaphore_signal(barrier, inc=1, device_id=(lax.rem(s + k, NS), h), device_id_type=MESH)
        return 0

    def greet_head(k, _):
        pl.semaphore_signal(barrier, inc=1, device_id=(s, lax.rem(h + k, NH)), device_id_type=MESH)
        return 0

    lax.fori_loop(1, NS, greet_seq, 0)
    lax.fori_loop(1, NH, greet_head, 0)
    for copy in small[:3]:
        copy.start()
    for i in range(LOOK):
        for copy in chunk_copies(i):
            copy.start()
    for copy in small[3:]:
        copy.start()
    acc[...] = jnp.zeros_like(acc)

    for copy in small[:3]:
        copy.wait()
    own_rows = jnp.concatenate([drows[i].astype(jnp.float32) for i in range(REQ)], axis=0).astype(jnp.bfloat16)
    for n in range(PER):
        drow_stage[n] = own_rows[:, n * KC : (n + 1) * KC]
        x[PER * h + n, TOK:ROWS, :] = own_rows[:, n * KC : (n + 1) * KC]
    dealt[s] = piece[s]
    pl.semaphore_wait(barrier, NS - 1 + NH - 1)

    def rows_copy(peer, owner, k):
        return pltpu.make_async_remote_copy(
            src_ref=drow_stage,
            dst_ref=x.at[pl.ds(PER * owner, PER), pl.ds(TOK, ROWS - TOK), :],
            send_sem=rows_send.at[k],
            recv_sem=rows_recv.at[owner],
            device_id=(s, peer),
            device_id_type=MESH,
        )

    def deal_copy(peer, owner):
        return pltpu.make_async_remote_copy(
            src_ref=piece.at[peer],
            dst_ref=dealt.at[owner],
            send_sem=deal_send.at[peer],
            recv_sem=deal_recv.at[owner],
            device_id=(peer, h),
            device_id_type=MESH,
        )

    def pick_copy(peer, owner):
        return pltpu.make_async_remote_copy(
            src_ref=picked.at[peer],
            dst_ref=prefix.at[owner],
            send_sem=pick_send.at[peer],
            recv_sem=pick_recv.at[owner],
            device_id=(peer, h),
            device_id_type=MESH,
        )

    def result_copy(peer, owner):
        return pltpu.make_async_remote_copy(
            src_ref=dec_send.at[peer],
            dst_ref=dec_recv.at[owner],
            send_sem=res_send.at[peer],
            recv_sem=res_recv.at[owner],
            device_id=(peer, h),
            device_id_type=MESH,
        )

    def over_seq(act):
        def step(k, _):
            act(lax.rem(s + k, NS))
            return 0

        lax.fori_loop(1, NS, step, 0)

    def send_rows(k, _):
        rows_copy(lax.rem(h + NH - k, NH), h, k).start()
        return 0

    over_seq(lambda peer: deal_copy(peer, s).start())
    lax.fori_loop(1, NH, send_rows, 0)

    def pick():
        over_seq(lambda peer: deal_copy(s, peer).wait_recv())

        def one(d, _):
            for j in range(REQ):
                picked[d, j] = dealt[soft_s[REQ * d + j]]
            return 0

        lax.fori_loop(0, NS, one, 0)
        prefix[s] = picked[s]
        over_seq(lambda peer: pick_copy(peer, s).start())

    def project(i, _):
        c = lax.rem(PER * h + i, NC)
        for copy in chunk_copies(i):
            copy.wait()

        @pl.when(jnp.logical_and(lax.rem(i, PER) == 0, i > 0))
        def _():
            owner = lax.rem(h + i // PER, NH)
            rows_copy(h, owner, 0).wait_recv()

        @pl.when(i < NC - LOOK)
        def _():
            for copy in chunk_copies(i + LOOK):
                copy.start()

        @pl.when(i == 5)
        def _():
            pick()

        for n in range(W // 256):
            at = slice(256 * n, 256 * n + 256)
            acc[:, at] += jnp.dot(x[c], w[c, :, at], preferred_element_type=jnp.float32)
        return 0

    for copy in small[3:]:
        copy.wait()
    lax.fori_loop(0, NC, project, 0)

    row_in_block = lax.broadcasted_iota(jnp.int32, (REQ * STEPS, HD), 0)
    cosine_d = jnp.concatenate([rope_v[0, pl.ds(len_s[REQ * s + i], STEPS), :] for i in range(REQ)], axis=0)
    sine_d = jnp.concatenate([rope_v[1, pl.ds(len_s[REQ * s + i], STEPS), :] for i in range(REQ)], axis=0)
    b_q = bq[...].astype(jnp.float32).reshape(1, QW)
    b_k = bk[...].astype(jnp.float32).reshape(1, HD)
    b_v = bv[...].astype(jnp.float32).reshape(1, HD)
    for j in range(GROUP):
        at = slice(HD * j, HD * j + HD)
        rotated = rotate(acc[TOK:ROWS, at] + b_q[:, at], cosine_d, sine_d)
        dec_f32[...] = rotated
        for i in range(REQ):
            dq[i, STEPS * j : STEPS * j + STEPS, :] = dec_f32[STEPS * i : STEPS * i + STEPS, :]
    dk[...] = rotate(acc[TOK:ROWS, QW : QW + HD] + b_k, cosine_d, sine_d).astype(jnp.bfloat16)
    dv[...] = (acc[TOK:ROWS, QW + HD : W] + b_v).astype(jnp.bfloat16)

    cosine = rope_v[0, 0:PAGE, :]
    sine = rope_v[1, 0:PAGE, :]

    def finish(p, _):
        rows = pl.ds(pl.multiple_of(p * PAGE, PAGE), PAGE)
        keys[p] = rotate(acc[rows, QW : QW + HD] + b_k, cosine, sine).astype(jnp.bfloat16)
        values[p] = (acc[rows, QW + HD : W] + b_v).astype(jnp.bfloat16)
        for j in range(GROUP):
            at = slice(HD * j, HD * j + HD)
            queries[p, HD * j : HD * j + HD, :] = rotate(acc[rows, at] + b_q[:, at], cosine, sine).astype(jnp.bfloat16)
        return 0

    lax.fori_loop(0, REQ, finish, 0)
    over_seq(lambda peer: pick_copy(s, peer).wait_recv())

    ones = jnp.ones((PFX + 2 * PAGE, HD), jnp.bfloat16)
    value_all[:, HD:] = ones
    col = lax.broadcasted_iota(jnp.int32, (GROUP * STEPS, PFX + 2 * PAGE), 1)
    row = lax.broadcasted_iota(jnp.int32, (GROUP * STEPS, PFX + 2 * PAGE), 0)
    for i in range(REQ):
        page = jnp.clip(table_s[REQ * s + i] - REQ * s, 0, REQ - 1)
        key_all[0:PFX, :] = prefix[:, i, 0:PIECE, :].reshape(PFX, HD)
        value_all[0:PFX, 0:HD] = prefix[:, i, PIECE : 2 * PIECE, :].reshape(PFX, HD)
        key_all[PFX : PFX + PAGE, :] = keys[page]
        value_all[PFX : PFX + PAGE, 0:HD] = values[page]
        key_all[PFX + PAGE : PFX + PAGE + REQ * STEPS, :] = dk[...]
        value_all[PFX + PAGE : PFX + PAGE + REQ * STEPS, 0:HD] = dv[...]
        if i == 0:
            empty = PFX + PAGE + REQ * STEPS
            key_all[empty:, :] = jnp.zeros((PFX + 2 * PAGE - empty, HD), jnp.bfloat16)
            value_all[empty:, 0:HD] = jnp.zeros((PFX + 2 * PAGE - empty, HD), jnp.bfloat16)
        first = PFX + PAGE + STEPS * i
        live = (col < PFX + len_s[REQ * s + i]) | ((col >= first) & (col - first <= lax.rem(row, STEPS)))
        score = jnp.where(live, scores_of(dq[i].astype(jnp.bfloat16), key_all[...]), -1e30)
        weight = jnp.exp2((score - jnp.max(score, axis=1, keepdims=True)) * EXP2_SCALE).astype(jnp.bfloat16)
        total = jnp.dot(weight, value_all[...], preferred_element_type=jnp.float32)
        dec_res[i] = (total[:, 0:HD] / total[:, HD:]).astype(jnp.bfloat16)

    def route(o, _):
        which = 0
        for c in range(SLOTS):
            offset = plan_s[SLOTS * o + c] - REQ * s
            which += jnp.where((offset >= 0) & (offset < REQ), offset, 0)
        dec_send[o] = dec_res[jnp.minimum(which, REQ - 1)]
        return 0

    lax.fori_loop(0, NS, route, 0)
    dec_recv[s] = dec_send[s]
    over_seq(lambda peer: result_copy(peer, s).start())

    causal = jnp.where(
        lax.broadcasted_iota(jnp.int32, (PAGE, PAGE), 1) <= lax.broadcasted_iota(jnp.int32, (PAGE, PAGE), 0), 0.0, -1e30
    )
    causal = jnp.concatenate([causal] * HEADS_AT_ONCE, axis=0)
    slot = lax.broadcasted_iota(jnp.int32, (PAGE, HD), 0)

    def out_copy(p):
        rows = pl.ds(pl.multiple_of(p * PAGE, PAGE), PAGE)
        return pltpu.make_async_copy(out_stage.at[rows, :], prefill_out.at[rows, :], out_sem.at[p])

    def attend(p, _):
        rows = pl.ds(pl.multiple_of(p * PAGE, PAGE), PAGE)
        holder, length = 0, 0
        for i in range(REQ):
            mine = table_s[REQ * s + i] == REQ * s + p
            holder += jnp.where(mine, i, 0)
            length += jnp.where(mine, len_s[REQ * s + i], 0)
        holder = jnp.minimum(holder, REQ - 1)
        key_all[0:PFX, :] = prefix[:, holder, 0:PIECE, :].reshape(PFX, HD)
        value_all[0:PFX, 0:HD] = prefix[:, holder, PIECE : 2 * PIECE, :].reshape(PFX, HD)
        key_all[PFX : PFX + PAGE, :] = keys[p]
        value_all[PFX : PFX + PAGE, 0:HD] = values[p]
        for g in range(GROUP // HEADS_AT_ONCE):
            n = HEADS_AT_ONCE * HD
            query = queries[p, g * n : (g + 1) * n, :]
            score = scores_of(query, key_all[0 : PFX + PAGE, :])
            fixed, own = score[:, 0:PFX], score[:, PFX:] + causal
            top = jnp.maximum(jnp.max(fixed, axis=1, keepdims=True), jnp.max(own, axis=1, keepdims=True))
            fixed = jnp.exp2((fixed - top) * EXP2_SCALE).astype(jnp.bfloat16)
            own = jnp.exp2((own - top) * EXP2_SCALE).astype(jnp.bfloat16)
            total = jnp.dot(
                jnp.concatenate([fixed, own], axis=1), value_all[0 : PFX + PAGE, :], preferred_element_type=jnp.float32
            )
            result = total[:, 0:HD] / total[:, HD:]
            for j in range(HEADS_AT_ONCE):
                at = (g * HEADS_AT_ONCE + j) * HD
                out_stage[rows, at : at + HD] = jnp.where(
                    slot < length, result[HD * j : HD * j + HD, :], 0.0
                ).astype(jnp.bfloat16)
        out_copy(p).start()
        return 0

    lax.fori_loop(0, REQ, attend, 0)

    over_seq(lambda peer: result_copy(s, peer).wait_recv())
    for c in range(SLOTS):
        request = plan_s[SLOTS * s + c]
        live = jnp.where(request >= 0, 1.0, 0.0)
        dq[0] = dec_recv[jnp.maximum(request, 0) // REQ].astype(jnp.float32) * live
        dec_out_v[c] = jnp.concatenate(
            [dq[0, STEPS * j : STEPS * j + STEPS, :] for j in range(GROUP)], axis=1
        ).astype(jnp.bfloat16)
    done = pltpu.make_async_copy(dec_out_v, decode_out, small_sem.at[0])
    done.start()

    def drain(k, _):
        rows_copy(h, h, k).wait_send()
        return 0

    lax.fori_loop(1, NH, drain, 0)
    over_seq(lambda peer: deal_copy(peer, s).wait_send())
    over_seq(lambda peer: pick_copy(peer, s).wait_send())
    over_seq(lambda peer: result_copy(peer, s).wait_send())
    for p in range(REQ):
        out_copy(p).wait()
    done.wait()


def body(*operands):
    (tokens, w_query, w_key, w_value, b_query, b_key, b_value, prefix_keys, prefix_values, decode_rows, *tables) = operands
    bf16, f32, i32 = jnp.bfloat16, jnp.float32, jnp.int32
    dma = pltpu.SemaphoreType.DMA
    return pl.pallas_call(
        kernel,
        out_shape=(
            jax.ShapeDtypeStruct((TOK, QW), bf16),
            jax.ShapeDtypeStruct((SLOTS, STEPS, QW), bf16),
        ),
        in_specs=[pl.BlockSpec(memory_space=pl.ANY)] * 15,
        out_specs=(pl.BlockSpec(memory_space=pl.ANY), pl.BlockSpec(memory_space=pl.ANY)),
        scratch_shapes=[
            pltpu.VMEM((NC, ROWS, KC), bf16),
            pltpu.VMEM((NC, KC, W), bf16),
            pltpu.VMEM((ROWS, W), f32),
            pltpu.VMEM((REQ, GROUP * PAGE, HD), bf16),
            pltpu.VMEM((REQ, PAGE, HD), bf16),
            pltpu.VMEM((REQ, PAGE, HD), bf16),
            pltpu.VMEM((PFX + 2 * PAGE, HD), bf16),
            pltpu.VMEM((PFX + 2 * PAGE, 2 * HD), bf16),
            pltpu.VMEM((TOK, QW), bf16),
            pltpu.VMEM((QW,), bf16),
            pltpu.VMEM((HD,), bf16),
            pltpu.VMEM((HD,), bf16),
            pltpu.VMEM((2, ROPE_ROWS, HD), f32),
            pltpu.VMEM((REQ, STEPS, D // NH), bf16),
            pltpu.VMEM((PER, ROWS - TOK, KC), bf16),
            pltpu.VMEM((NS, 2 * PIECE, HD), bf16),
            pltpu.VMEM((NS, 2 * PIECE, HD), bf16),
            pltpu.VMEM((NS, REQ, 2 * PIECE, HD), bf16),
            pltpu.VMEM((NS, REQ, 2 * PIECE, HD), bf16),
            pltpu.VMEM((REQ, GROUP * STEPS, HD), f32),
            pltpu.VMEM((REQ * STEPS, HD), bf16),
            pltpu.VMEM((REQ * STEPS, HD), bf16),
            pltpu.VMEM((REQ * STEPS, HD), bf16),
            pltpu.VMEM((REQ * STEPS, HD), bf16),
            pltpu.VMEM((REQ * STEPS, HD), f32),
            pltpu.VMEM((REQ, GROUP * STEPS, HD), bf16),
            pltpu.VMEM((NS, GROUP * STEPS, HD), bf16),
            pltpu.VMEM((NS, GROUP * STEPS, HD), bf16),
            pltpu.VMEM((SLOTS, STEPS, QW), bf16),
            pltpu.SMEM((64,), i32),
            pltpu.SMEM((64,), i32),
            pltpu.SMEM((64,), i32),
            pltpu.SMEM((128,), i32),
            dma((4, NC)),
            dma((11,)),
            dma((REQ,)),
            dma((NH,)),
            dma((NH,)),
            dma((NS,)),
            dma((NS,)),
            dma((NS,)),
            dma((NS,)),
            dma((NS,)),
            dma((NS,)),
        ],
        compiler_params=pltpu.CompilerParams(
            collective_id=0, has_side_effects=True, vmem_limit_bytes=56 * 1024 * 1024
        ),
        name="layer",
    )(
        tokens,
        w_query,
        w_key,
        w_value,
        b_query,
        b_key,
        b_value,
        prefix_keys.reshape(NS, PIECE, HD),
        prefix_values.reshape(NS, PIECE, HD),
        decode_rows,
        *tables,
        jnp.asarray(rope_table()),
    )


def solution(mesh):
    in_specs = (
        P("seq", None),
        P(None, "head"),
        P(None, "head"),
        P(None, "head"),
        P("head"),
        P("head"),
        P("head"),
        P("seq", None, "head"),
        P("seq", None, "head"),
        P("seq", None, "head"),
        P(),
        P(),
        P(),
        P(),
    )
    out_specs = (P("seq", "head"), P("seq", None, "head"))
    return jax.shard_map(body, mesh=mesh, in_specs=in_specs, out_specs=out_specs, check_vma=False)
```

time: 205 us -> 38.9 us (0.19)
  the two profiles are of different devices: /device:TPU:0 before, /device:TPU:1 now
where the time goes in v1:
time: 38.9 us; the launch traced here: 38.7 us
  Pallas kernels  34.3 us (88%)
  local copies, waits for them, and re-layouts  3.75 us (10%)
  between operations  0.64 us (2%)
    pallas_call x1, Pallas kernels, body(): pl.pallas_call(kernel, out_shape=(jax.ShapeDtypeStruct((TOK, QW), bf16),...  34.3 us
    unnamed x2, local copies, waits for them, and re-layouts  3.75 us

profile of v1, /device:TPU:1, one launch (start us, length us, event | category | flops | bytes accessed | tf_op | source)
XLA Modules:
  0.0 38.7 jit_solution(10096203600794616639)
XLA Ops:
  0.6 34.3 %layer.1 = (bf16[512,1024]{1,0:T(8,128)(2,1)}, bf16[8,4,1024]{2,1,0:T(4,128)(2,1)}) custom-call(bf16[512,8192]{1,0:T(8,128)(2,1)} %tokens.1, bf16[8192,1024]{1,0:T(8,128)(2,1)} %w_query.1, bf16[8192,128]{1,0:T(8,128)(2,1)} %w_key.1, bf16[8192,128]{1,0:T(8,128)(2,1)} %w_value.1, bf16[1024]{0:T(1024)(128)(2,1)} %b_query.1, bf16[128]{0:T(256)(128)(2,1)} %b_key.1, ...), custom_call_target="tpu_custom_call" | custom-call | tf_op jit(solution)/shard_map/layer/pallas_call | solution.py:356
  34.9 2.3 %copy.19 = bf16[512,1024]{1,0:T(8,128)(2,1)} copy(bf16[512,1024]{1,0:T(8,128)(2,1)} %get-tuple-element.4) | data formatting | bytes 2097152
  37.2 1.5 %copy.20 = bf16[8,4,1024]{2,1,0:T(4,128)(2,1)} copy(bf16[8,4,1024]{2,1,0:T(4,128)(2,1)} %get-tuple-element.5) | data formatting | bytes 131072

commit v2 on v1

v2 whole, which is shorter than its diff:
```python
import functools
import math

import jax
import jax.numpy as jnp
import numpy as np
from jax import lax
from jax.experimental import pallas as pl
from jax.experimental.pallas import tpu as pltpu
from jax.sharding import PartitionSpec as P

HD = 128
PAGE = 128
PFX = 256
STEPS = 4
REQ = 4
SLOTS = 8
NS = 16
NH = 8
GROUP = 8
D = 8192
TOK = REQ * PAGE
DROWS = REQ * STEPS
ROWS = TOK + DROWS
QW = GROUP * HD
W = QW + 2 * HD
FEAT = D // NH
HALF = FEAT // 2
LOOK = 2
PICK_BLOCK = 2
PIECE = PFX // NS
KEYS = PFX + PAGE
ALL_KEYS = KEYS + PAGE
MESH = pl.DeviceIdType.MESH
EXP2_SCALE = math.log2(math.e) / math.sqrt(HD)
ROPE_ROWS = 136


def rope_table():
    frequency = 1000000.0 ** (-np.arange(HD // 2, dtype=np.float64) * 2.0 / HD)
    angles = (PFX + np.arange(ROPE_ROWS, dtype=np.float64))[:, None] * frequency
    cosine = np.concatenate([np.cos(angles), np.cos(angles)], axis=1)
    sine = np.concatenate([-np.sin(angles), np.sin(angles)], axis=1)
    return np.stack([cosine, sine]).astype(np.float32)


def rotate(vectors, cosine, sine):
    return vectors * cosine + pltpu.roll(vectors, HD // 2, 1) * sine


def scores_of(queries, keys):
    return lax.dot_general(queries, keys, (((1,), (1,)), ((), ())), preferred_element_type=jnp.float32)


def softmax_product(score, values_and_ones):
    weight = jnp.exp2((score - jnp.max(score, axis=1, keepdims=True)) * EXP2_SCALE).astype(jnp.bfloat16)
    total = jnp.dot(weight, values_and_ones, preferred_element_type=jnp.float32)
    return total[:, 0:HD] * pltpu.reciprocal(total[:, HD:], approx=True)


def kernel(
    tokens, w_query, w_key, w_value, b_query, b_key, b_value, prefix_keys, prefix_values, decode_rows,
    page_table, prompt_len, soft_ids, plan, rope,
    prompt_res, decode_res,
    x, w, acc, key_all, value_all,
    bq, bk, bv, rope_v, drows, piece, dealt, picked, prefix, dq, dec_f32, dec_res, dec_send, dec_recv,
    table_s, len_s, soft_s, plan_s,
    chunk_sem, small_sem, rows_send, rows_recv, deal_send, deal_recv, pick_send, pick_recv, res_send, res_recv,
):
    s = lax.axis_index("seq")
    h = lax.axis_index("head")

    def piece_copies(n, block, start, length):
        source = pl.multiple_of(lax.rem(h + block, NH) * FEAT + start, length)
        here = pl.ds(pl.multiple_of(block * FEAT + start, length), length)
        at = pl.ds(source, length)
        return (
            pltpu.make_async_copy(tokens.at[:, at], x.at[pl.ds(0, TOK), here], chunk_sem.at[0, n]),
            pltpu.make_async_copy(w_query.at[at, :], w.at[here, pl.ds(0, QW)], chunk_sem.at[1, n]),
            pltpu.make_async_copy(w_key.at[at, :], w.at[here, pl.ds(QW, HD)], chunk_sem.at[2, n]),
            pltpu.make_async_copy(w_value.at[at, :], w.at[here, pl.ds(QW + HD, HD)], chunk_sem.at[3, n]),
        )

    halves = (piece_copies(0, 0, 0, HALF), piece_copies(NH, 0, HALF, HALF))

    def block_copies(b):
        return piece_copies(b, b, 0, FEAT)

    def start(copies):
        for copy in copies:
            copy.start()

    def wait(copies):
        for copy in copies:
            copy.wait()

    small = [
        pltpu.make_async_copy(src, dst, small_sem.at[n])
        for n, (src, dst) in enumerate(
            (
                (decode_rows, drows),
                (prefix_keys, piece.at[:, pl.ds(0, PIECE), :]),
                (prefix_values, piece.at[:, pl.ds(PIECE, PIECE), :]),
                (soft_ids, soft_s),
                (page_table, table_s),
                (prompt_len, len_s),
                (plan, plan_s),
                (b_query, bq),
                (b_key, bk),
                (b_value, bv),
                (rope, rope_v),
            )
        )
    ]

    def over_seq(act):
        def step(k, _):
            act(lax.rem(s + k, NS))
            return 0

        lax.fori_loop(1, NS, step, 0)

    def over_head(act):
        def step(k, _):
            act(k)
            return 0

        lax.fori_loop(1, NH, step, 0)

    def rows_copy(b):
        return pltpu.make_async_remote_copy(
            src_ref=x.at[pl.ds(TOK, DROWS), pl.ds(0, FEAT)],
            dst_ref=x.at[pl.ds(TOK, DROWS), pl.ds(pl.multiple_of(b * FEAT, FEAT), FEAT)],
            send_sem=rows_send.at[b],
            recv_sem=rows_recv.at[b],
            device_id=(s, lax.rem(h + NH - b, NH)),
            device_id_type=MESH,
        )

    def seq_copy(source, target, send, recv):
        def copy(peer, owner):
            return pltpu.make_async_remote_copy(
                src_ref=source.at[peer],
                dst_ref=target.at[owner],
                send_sem=send.at[peer],
                recv_sem=recv.at[owner],
                device_id=(peer, h),
                device_id_type=MESH,
            )

        return copy

    deal_copy = seq_copy(piece, dealt, deal_send, deal_recv)
    pick_copy = seq_copy(picked, prefix, pick_send, pick_recv)
    result_copy = seq_copy(dec_send, dec_recv, res_send, res_recv)

    barrier = pltpu.get_barrier_semaphore()

    def greet(peer):
        pl.semaphore_signal(barrier, inc=1, device_id=peer, device_id_type=MESH)

    over_seq(lambda peer: greet((peer, h)))
    over_head(lambda k: greet((s, lax.rem(h + k, NH))))
    start(small[:3])
    start(halves[0])
    start(halves[1])
    start(small[3:])
    for b in range(1, LOOK):
        start(block_copies(b))

    small[0].wait()
    x[TOK:ROWS, 0:FEAT] = jnp.concatenate([drows[i].astype(jnp.float32) for i in range(REQ)], axis=0).astype(jnp.bfloat16)
    pl.semaphore_wait(barrier, NS - 1 + NH - 1)
    over_head(lambda b: rows_copy(b).start())
    for copy in small[1:3]:
        copy.wait()
    dealt[s] = piece[s]
    over_seq(lambda peer: deal_copy(peer, s).start())

    def pick():
        over_seq(lambda peer: deal_copy(s, peer).wait_recv())

        def one(d, _):
            for j in range(REQ):
                picked[d, j] = dealt[soft_s[REQ * d + j]]
            return 0

        lax.fori_loop(0, NS, one, 0)
        prefix[s] = picked[s]
        over_seq(lambda peer: pick_copy(peer, s).start())

    def project(begin, length, add):
        at = pl.ds(begin, length)
        for n in range(W // 256):
            to = slice(256 * n, 256 * n + 256)
            product = jnp.dot(x[:, at], w[at, to], preferred_element_type=jnp.float32)
            if add:
                acc[:, to] += product
            else:
                acc[:, to] = product

    def project_block(b, _):
        wait(block_copies(b))
        rows_copy(b).wait_recv()

        @pl.when(b + LOOK < NH)
        def _():
            start(block_copies(b + LOOK))

        @pl.when(b == PICK_BLOCK)
        def _():
            pick()

        project(pl.multiple_of(b * FEAT, FEAT), FEAT, True)
        return 0

    wait(halves[0])
    project(0, HALF, False)
    wait(halves[1])
    start(block_copies(LOOK))
    project(HALF, HALF, True)
    wait(small[3:])
    lax.fori_loop(1, NH, project_block, 0)

    b_q = bq[...].astype(jnp.float32).reshape(1, QW)
    b_k = bk[...].astype(jnp.float32).reshape(1, HD)
    b_v = bv[...].astype(jnp.float32).reshape(1, HD)
    cosine = rope_v[0, 0:PAGE, :]
    sine = rope_v[1, 0:PAGE, :]

    holder, length = [], []
    for p in range(REQ):
        who, live = 0, 0
        for i in range(REQ):
            mine = table_s[REQ * s + i] == REQ * s + p
            who += jnp.where(mine, i, 0)
            live += jnp.where(mine, len_s[REQ * s + i], 0)
        holder.append(jnp.minimum(who, REQ - 1))
        length.append(live)

    cosine_d = jnp.concatenate([rope_v[0, pl.ds(len_s[REQ * s + i], STEPS), :] for i in range(REQ)], axis=0)
    sine_d = jnp.concatenate([rope_v[1, pl.ds(len_s[REQ * s + i], STEPS), :] for i in range(REQ)], axis=0)
    for j in range(GROUP):
        at = slice(HD * j, HD * j + HD)
        dec_f32[j, 0:DROWS, :] = rotate(acc[TOK:ROWS, at] + b_q[:, at], cosine_d, sine_d)
        for i in range(REQ):
            dq[i, STEPS * j : STEPS * j + STEPS, :] = dec_f32[j, STEPS * i : STEPS * i + STEPS, :]
    step_keys = rotate(acc[TOK:ROWS, QW : QW + HD] + b_k, cosine_d, sine_d).astype(jnp.bfloat16)
    step_values = (acc[TOK:ROWS, QW + HD : W] + b_v).astype(jnp.bfloat16)
    step_keys = jnp.concatenate([step_keys, jnp.zeros((PAGE - DROWS, HD), jnp.bfloat16)], axis=0)
    step_values = jnp.concatenate([step_values, jnp.zeros((PAGE - DROWS, HD), jnp.bfloat16)], axis=0)

    for p in range(REQ):
        rows = slice(PAGE * p, PAGE * p + PAGE)
        key_all[p, PFX:KEYS, :] = rotate(acc[rows, QW : QW + HD] + b_k, cosine, sine).astype(jnp.bfloat16)
        value_all[p, PFX:KEYS, 0:HD] = (acc[rows, QW + HD : W] + b_v).astype(jnp.bfloat16)
        key_all[p, KEYS:, :] = step_keys
        value_all[p, KEYS:, 0:HD] = step_values
        value_all[p, :, HD:] = jnp.ones((ALL_KEYS, HD), jnp.bfloat16)
    over_seq(lambda peer: pick_copy(s, peer).wait_recv())
    for p in range(REQ):
        key_all[p, 0:PFX, :] = prefix[:, holder[p], 0:PIECE, :].reshape(PFX, HD)
        value_all[p, 0:PFX, 0:HD] = prefix[:, holder[p], PIECE : 2 * PIECE, :].reshape(PFX, HD)

    col = lax.broadcasted_iota(jnp.int32, (GROUP * STEPS, ALL_KEYS), 1)
    step = lax.rem(lax.broadcasted_iota(jnp.int32, (GROUP * STEPS, ALL_KEYS), 0), STEPS)
    for p in range(REQ):
        own = col - (KEYS + STEPS * holder[p])
        live = (col < PFX + length[p]) | ((own >= 0) & (own <= step))
        score = jnp.where(live, scores_of(dq[holder[p]].astype(jnp.bfloat16), key_all[p]), -1e30)
        dec_res[p] = softmax_product(score, value_all[p]).astype(jnp.bfloat16)

    def route(o, _):
        which = 0
        for c in range(SLOTS):
            offset = plan_s[SLOTS * o + c] - REQ * s
            which += jnp.where((offset >= 0) & (offset < REQ), offset, 0)
        page = table_s[REQ * s + jnp.minimum(which, REQ - 1)] - REQ * s
        dec_send[o] = dec_res[jnp.clip(page, 0, REQ - 1)]
        return 0

    lax.fori_loop(0, NS, route, 0)
    dec_recv[s] = dec_send[s]
    over_seq(lambda peer: result_copy(peer, s).start())

    causal = jnp.where(
        lax.broadcasted_iota(jnp.int32, (PAGE, PAGE), 1) <= lax.broadcasted_iota(jnp.int32, (PAGE, PAGE), 0), 0.0, -1e30
    )
    causal = jnp.concatenate([causal] * GROUP, axis=0)
    slot = lax.broadcasted_iota(jnp.int32, (PAGE, HD), 0)
    for p in range(REQ):
        rows = slice(PAGE * p, PAGE * p + PAGE)
        query = jnp.concatenate(
            [
                rotate(acc[rows, HD * j : HD * j + HD] + b_q[:, HD * j : HD * j + HD], cosine, sine).astype(jnp.bfloat16)
                for j in range(GROUP)
            ],
            axis=0,
        )
        score = scores_of(query, key_all[p, 0:KEYS, :])
        score = jnp.concatenate([score[:, 0:PFX], score[:, PFX:] + causal], axis=1)
        result = softmax_product(score, value_all[p, 0:KEYS, :])
        for j in range(GROUP):
            prompt_res[rows, HD * j : HD * j + HD] = jnp.where(
                slot < length[p], result[PAGE * j : PAGE * j + PAGE, :], 0.0
            ).astype(jnp.bfloat16)

    over_seq(lambda peer: result_copy(s, peer).wait_recv())
    for c in range(SLOTS):
        request = plan_s[SLOTS * s + c]
        live = jnp.where(request >= 0, 1.0, 0.0)
        dec_f32[c] = dec_recv[jnp.maximum(request, 0) // REQ].astype(jnp.float32) * live
        decode_res[c] = jnp.concatenate(
            [dec_f32[c, STEPS * j : STEPS * j + STEPS, :] for j in range(GROUP)], axis=1
        ).astype(jnp.bfloat16)

    over_head(lambda b: rows_copy(b).wait_send())
    over_seq(lambda peer: deal_copy(peer, s).wait_send())
    over_seq(lambda peer: pick_copy(peer, s).wait_send())
    over_seq(lambda peer: result_copy(peer, s).wait_send())


def store_kernel(prompt_res, decode_res, prefill_out, decode_out, sem):
    copies = (
        pltpu.make_async_copy(prompt_res, prefill_out, sem.at[0]),
        pltpu.make_async_copy(decode_res, decode_out, sem.at[1]),
    )
    for copy in copies:
        copy.start()
    for copy in copies:
        copy.wait()


def body(*operands):
    (tokens, w_query, w_key, w_value, b_query, b_key, b_value, prefix_keys, prefix_values, decode_rows, *tables) = operands
    bf16, f32, i32 = jnp.bfloat16, jnp.float32, jnp.int32
    dma = pltpu.SemaphoreType.DMA
    anywhere = pl.BlockSpec(memory_space=pl.ANY)
    results = pl.pallas_call(
        kernel,
        out_shape=(pltpu.VMEM((TOK, QW), bf16), pltpu.VMEM((SLOTS, STEPS, QW), bf16)),
        in_specs=[anywhere] * 15,
        scratch_shapes=[
            pltpu.VMEM((ROWS, D), bf16),
            pltpu.VMEM((D, W), bf16),
            pltpu.VMEM((ROWS, W), f32),
            pltpu.VMEM((REQ, ALL_KEYS, HD), bf16),
            pltpu.VMEM((REQ, ALL_KEYS, 2 * HD), bf16),
            pltpu.VMEM((QW,), bf16),
            pltpu.VMEM((HD,), bf16),
            pltpu.VMEM((HD,), bf16),
            pltpu.VMEM((2, ROPE_ROWS, HD), f32),
            pltpu.VMEM((REQ, STEPS, FEAT), bf16),
            pltpu.VMEM((NS, 2 * PIECE, HD), bf16),
            pltpu.VMEM((NS, 2 * PIECE, HD), bf16),
            pltpu.VMEM((NS, REQ, 2 * PIECE, HD), bf16),
            pltpu.VMEM((NS, REQ, 2 * PIECE, HD), bf16),
            pltpu.VMEM((REQ, GROUP * STEPS, HD), f32),
            pltpu.VMEM((GROUP, GROUP * STEPS, HD), f32),
            pltpu.VMEM((REQ, GROUP * STEPS, HD), bf16),
            pltpu.VMEM((NS, GROUP * STEPS, HD), bf16),
            pltpu.VMEM((NS, GROUP * STEPS, HD), bf16),
            pltpu.SMEM((64,), i32),
            pltpu.SMEM((64,), i32),
            pltpu.SMEM((64,), i32),
            pltpu.SMEM((128,), i32),
            dma((4, NH + 1)),
            dma((11,)),
            dma((NH,)),
            dma((NH,)),
            dma((NS,)),
            dma((NS,)),
            dma((NS,)),
            dma((NS,)),
            dma((NS,)),
            dma((NS,)),
        ],
        compiler_params=pltpu.CompilerParams(
            collective_id=0, has_side_effects=True, vmem_limit_bytes=56 * 1024 * 1024
        ),
        name="layer",
    )(
        tokens,
        w_query,
        w_key,
        w_value,
        b_query,
        b_key,
        b_value,
        prefix_keys.reshape(NS, PIECE, HD),
        prefix_values.reshape(NS, PIECE, HD),
        decode_rows,
        *tables,
        jnp.asarray(rope_table()),
    )
    return pl.pallas_call(
        store_kernel,
        out_shape=(jax.ShapeDtypeStruct((TOK, QW), bf16), jax.ShapeDtypeStruct((SLOTS, STEPS, QW), bf16)),
        in_specs=[pl.BlockSpec(memory_space=pltpu.VMEM)] * 2,
        out_specs=(anywhere, anywhere),
        scratch_shapes=[dma((2,))],
        compiler_params=pltpu.CompilerParams(vmem_limit_bytes=8 * 1024 * 1024),
        name="store",
    )(*results)


def solution(mesh):
    in_specs = (
        P("seq", None),
        P(None, "head"),
        P(None, "head"),
        P(None, "head"),
        P("head"),
        P("head"),
        P("head"),
        P("seq", None, "head"),
        P("seq", None, "head"),
        P("seq", None, "head"),
        P(),
        P(),
        P(),
        P(),
    )
    out_specs = (P("seq", "head"), P("seq", None, "head"))
    return jax.shard_map(body, mesh=mesh, in_specs=in_specs, out_specs=out_specs, check_vma=False)
```

time: 38.9 us -> 32.9 us (0.85)
  the two profiles are of different devices: /device:TPU:1 before, /device:TPU:0 now
where the time goes in v2:
time: 32.9 us; the launch traced here: 32.8 us
  Pallas kernels  32.2 us (98%)
  between operations  0.64 us (2%)
    pallas_call x1, Pallas kernels, body(): pl.pallas_call(kernel, out_shape=(pltpu.VMEM((TOK, QW), bf16), pltpu.VMEM...  31.2 us
    pallas_call x1, Pallas kernels, body(): pl.pallas_call(store_kernel, out_shape=(jax.ShapeDtypeStruct((TOK, QW), b...  0.99 us

profile of v2, /device:TPU:0, one launch (start us, length us, event | category | flops | bytes accessed | tf_op | source)
XLA Modules:
  0.0 32.8 jit_solution(11734042679974270988)
XLA Ops:
  0.6 31.2 %layer.1 = (bf16[512,1024]{1,0:T(8,128)(2,1)S(1)}, bf16[8,4,1024]{2,1,0:T(4,128)(2,1)S(1)}) custom-call(bf16[512,8192]{1,0:T(8,128)(2,1)} %tokens.1, bf16[8192,1024]{1,0:T(8,128)(2,1)} %w_query.1, bf16[8192,128]{1,0:T(8,128)(2,1)} %w_key.1, bf16[8192,128]{1,0:T(8,128)(2,1)} %w_value.1, bf16[1024]{0:T(1024)(128)(2,1)} %b_query.1, bf16[128]{0:T(256)(128)(2,1)} %b_key.1, ...), custom_call_target="tpu_custom_call" | custom-call | tf_op jit(solution)/shard_map/layer/pallas_call | solution.py:339
  31.8 1.0 %store.1 = (bf16[512,1024]{1,0:T(8,128)(2,1)}, bf16[8,4,1024]{2,1,0:T(4,128)(2,1)}) custom-call(bf16[512,1024]{1,0:T(8,128)(2,1)S(1)} %get-tuple-element.4.prompt_res, bf16[8,4,1024]{2,1,0:T(4,128)(2,1)S(1)} %get-tuple-element.5.decode_res), custom_call_target="tpu_custom_call" | custom-call | tf_op jit(solution)/shard_map/store/pallas_call | solution.py:396

commit v3 on v2

--- a/solution.py
+++ b/solution.py
@@ -27,7 +27,10 @@
 FEAT = D // NH
 HALF = FEAT // 2
 LOOK = 2
-PICK_BLOCK = 2
+SEND_BLOCK = 1
+PICK_BLOCK = 3
+EARLY = 768
+LATE_DEPTH = 4096
 PIECE = PFX // NS
 KEYS = PFX + PAGE
 ALL_KEYS = KEYS + PAGE
@@ -62,7 +65,7 @@
     tokens, w_query, w_key, w_value, b_query, b_key, b_value, prefix_keys, prefix_values, decode_rows,
     page_table, prompt_len, soft_ids, plan, rope,
     prompt_res, decode_res,
-    x, w, acc, key_all, value_all,
+    x, rows_in, w, acc, key_all, value_all,
     bq, bk, bv, rope_v, drows, piece, dealt, picked, prefix, dq, dec_f32, dec_res, dec_send, dec_recv,
     table_s, len_s, soft_s, plan_s,
     chunk_sem, small_sem, rows_send, rows_recv, deal_send, deal_recv, pick_send, pick_recv, res_send, res_recv,
@@ -114,23 +117,17 @@
     ]
 
     def over_seq(act):
-        def step(k, _):
+        for k in range(1, NS):
             act(lax.rem(s + k, NS))
-            return 0
-
-        lax.fori_loop(1, NS, step, 0)
 
     def over_head(act):
-        def step(k, _):
-            act(k)
-            return 0
-
-        lax.fori_loop(1, NH, step, 0)
+        for b in range(1, NH):
+            act(b)
 
     def rows_copy(b):
         return pltpu.make_async_remote_copy(
-            src_ref=x.at[pl.ds(TOK, DROWS), pl.ds(0, FEAT)],
-            dst_ref=x.at[pl.ds(TOK, DROWS), pl.ds(pl.multiple_of(b * FEAT, FEAT), FEAT)],
+            src_ref=rows_in.at[:, pl.ds(0, FEAT)],
+            dst_ref=rows_in.at[:, pl.ds(pl.multiple_of(b * FEAT, FEAT), FEAT)],
             send_sem=rows_send.at[b],
             recv_sem=rows_recv.at[b],
             device_id=(s, lax.rem(h + NH - b, NH)),
@@ -168,14 +165,18 @@
     for b in range(1, LOOK):
         start(block_copies(b))
 
+    def deal():
+        pl.semaphore_wait(barrier, NS - 1 + NH - 1)
+        over_head(lambda b: rows_copy(b).start())
+        wait(small[1:3])
+        dealt[s] = piece[s]
+        over_seq(lambda peer: deal_copy(peer, s).start())
+
     small[0].wait()
-    x[TOK:ROWS, 0:FEAT] = jnp.concatenate([drows[i].astype(jnp.float32) for i in range(REQ)], axis=0).astype(jnp.bfloat16)
-    pl.semaphore_wait(barrier, NS - 1 + NH - 1)
-    over_head(lambda b: rows_copy(b).start())
-    for copy in small[1:3]:
-        copy.wait()
-    dealt[s] = piece[s]
-    over_seq(lambda peer: deal_copy(peer, s).start())
+    own_rows = jnp.concatenate([drows[i].astype(jnp.float32) for i in range(REQ)], axis=0).astype(jnp.bfloat16)
+    rows_in[:, 0:FEAT] = own_rows
+    x[TOK:ROWS, 0:FEAT] = own_rows
+    x[TOK:ROWS, FEAT : (SEND_BLOCK + 1) * FEAT] = jnp.zeros((DROWS, SEND_BLOCK * FEAT), jnp.bfloat16)
 
     def pick():
         over_seq(lambda peer: deal_copy(s, peer).wait_recv())
@@ -189,29 +190,42 @@
         prefix[s] = picked[s]
         over_seq(lambda peer: pick_copy(peer, s).start())
 
+    early = [(n, n + 256) for n in range(0, EARLY, 256)] + [(QW, W)]
+    late = [(n, n + 256) for n in range(EARLY, QW, 256)]
+
     def project(begin, length, add):
         at = pl.ds(begin, length)
-        for n in range(W // 256):
-            to = slice(256 * n, 256 * n + 256)
-            product = jnp.dot(x[:, at], w[at, to], preferred_element_type=jnp.float32)
-            if add:
-                acc[:, to] += product
-            else:
-                acc[:, to] = product
+        for rows, tiles in ((slice(0, ROWS), early), (slice(TOK, ROWS), late)):
+            for left, right in tiles:
+                product = jnp.dot(x[rows, at], w[at, left:right], preferred_element_type=jnp.float32)
+                if add:
+                    acc[rows, left:right] += product
+                else:
+                    acc[rows, left:right] = product
 
     def project_block(b, _):
         wait(block_copies(b))
-        rows_copy(b).wait_recv()
 
         @pl.when(b + LOOK < NH)
         def _():
             start(block_copies(b + LOOK))
 
+        @pl.when(b == SEND_BLOCK)
+        def _():
+            deal()
+
         @pl.when(b == PICK_BLOCK)
         def _():
             pick()
 
-        project(pl.multiple_of(b * FEAT, FEAT), FEAT, True)
+        at = pl.ds(pl.multiple_of(b * FEAT, FEAT), FEAT)
+
+        @pl.when(b > SEND_BLOCK)
+        def _():
+            rows_copy(b).wait_recv()
+            x[TOK:ROWS, at] = rows_in[:, at]
+
+        project(at.start, FEAT, True)
         return 0
 
     wait(halves[0])
@@ -221,6 +235,13 @@
     project(HALF, HALF, True)
     wait(small[3:])
     lax.fori_loop(1, NH, project_block, 0)
+
+    for b in range(1, SEND_BLOCK + 1):
+        rows_copy(b).wait_recv()
+    behind = slice(FEAT, (SEND_BLOCK + 1) * FEAT)
+    for n in range(0, W, 256):
+        to = slice(n, n + 256)
+        acc[TOK:ROWS, to] += jnp.dot(rows_in[:, behind], w[behind, to], preferred_element_type=jnp.float32)
 
     b_q = bq[...].astype(jnp.float32).reshape(1, QW)
     b_k = bk[...].astype(jnp.float32).reshape(1, HD)
@@ -286,24 +307,36 @@
     causal = jnp.where(
         lax.broadcasted_iota(jnp.int32, (PAGE, PAGE), 1) <= lax.broadcasted_iota(jnp.int32, (PAGE, PAGE), 0), 0.0, -1e30
     )
-    causal = jnp.concatenate([causal] * GROUP, axis=0)
     slot = lax.broadcasted_iota(jnp.int32, (PAGE, HD), 0)
-    for p in range(REQ):
+
+    def attend(p, heads):
         rows = slice(PAGE * p, PAGE * p + PAGE)
         query = jnp.concatenate(
             [
                 rotate(acc[rows, HD * j : HD * j + HD] + b_q[:, HD * j : HD * j + HD], cosine, sine).astype(jnp.bfloat16)
-                for j in range(GROUP)
+                for j in heads
             ],
             axis=0,
         )
         score = scores_of(query, key_all[p, 0:KEYS, :])
-        score = jnp.concatenate([score[:, 0:PFX], score[:, PFX:] + causal], axis=1)
-        result = softmax_product(score, value_all[p, 0:KEYS, :])
-        for j in range(GROUP):
+        own = score[:, PFX:] + jnp.concatenate([causal] * len(heads), axis=0)
+        result = softmax_product(jnp.concatenate([score[:, 0:PFX], own], axis=1), value_all[p, 0:KEYS, :])
+        for i, j in enumerate(heads):
             prompt_res[rows, HD * j : HD * j + HD] = jnp.where(
-                slot < length[p], result[PAGE * j : PAGE * j + PAGE, :], 0.0
+                slot < length[p], result[PAGE * i : PAGE * i + PAGE, :], 0.0
             ).astype(jnp.bfloat16)
+
+    acc[0:TOK, EARLY:QW] = jnp.zeros((TOK, QW - EARLY), jnp.float32)
+
+    def project_late(i, _):
+        at = pl.ds(pl.multiple_of(i * LATE_DEPTH, LATE_DEPTH), LATE_DEPTH)
+        for left, right in late:
+            acc[0:TOK, left:right] += jnp.dot(x[0:TOK, at], w[at, left:right], preferred_element_type=jnp.float32)
+        return 0
+
+    lax.fori_loop(0, D // LATE_DEPTH, project_late, 0)
+    for p in range(REQ):
+        attend(p, range(GROUP))
 
     over_seq(lambda peer: result_copy(s, peer).wait_recv())
     for c in range(SLOTS):
@@ -342,6 +375,7 @@
         in_specs=[anywhere] * 15,
         scratch_shapes=[
             pltpu.VMEM((ROWS, D), bf16),
+            pltpu.VMEM((DROWS, D), bf16),
             pltpu.VMEM((D, W), bf16),
             pltpu.VMEM((ROWS, W), f32),
             pltpu.VMEM((REQ, ALL_KEYS, HD), bf16),

time: 32.9 us -> 30.8 us (0.936)
  Pallas kernels: 32.2 us -> 30 us
    pallas_call x1, Pallas kernels: 31.2 us -> 29 us  [body(): pl.pallas_call(kernel, out_shape=(pltpu.VMEM((TOK, QW), bf16), pltpu.VMEM...]
where the time goes in v3:
time: 30.8 us; the launch traced here: 30.7 us
  Pallas kernels  30 us (97%)
  between operations  0.64 us (2%)
    pallas_call x1, Pallas kernels, body(): pl.pallas_call(kernel, out_shape=(pltpu.VMEM((TOK, QW), bf16), pltpu.VMEM...  29 us
    pallas_call x1, Pallas kernels, body(): pl.pallas_call(store_kernel, out_shape=(jax.ShapeDtypeStruct((TOK, QW), b...  0.99 us

profile of v3, /device:TPU:0, one launch (start us, length us, event | category | flops | bytes accessed | tf_op | source)
XLA Modules:
  0.0 30.7 jit_solution(12886056550059972799)
XLA Ops:
  0.6 29.0 %layer.1 = (bf16[512,1024]{1,0:T(8,128)(2,1)S(1)}, bf16[8,4,1024]{2,1,0:T(4,128)(2,1)S(1)}) custom-call(bf16[512,8192]{1,0:T(8,128)(2,1)} %tokens.1, bf16[8192,1024]{1,0:T(8,128)(2,1)} %w_query.1, bf16[8192,128]{1,0:T(8,128)(2,1)} %w_key.1, bf16[8192,128]{1,0:T(8,128)(2,1)} %w_value.1, bf16[1024]{0:T(1024)(128)(2,1)} %b_query.1, bf16[128]{0:T(256)(128)(2,1)} %b_key.1, ...), custom_call_target="tpu_custom_call" | custom-call | tf_op jit(solution)/shard_map/layer/pallas_call | solution.py:372
  29.7 1.0 %store.1 = (bf16[512,1024]{1,0:T(8,128)(2,1)}, bf16[8,4,1024]{2,1,0:T(4,128)(2,1)}) custom-call(bf16[512,1024]{1,0:T(8,128)(2,1)S(1)} %get-tuple-element.4.prompt_res, bf16[8,4,1024]{2,1,0:T(4,128)(2,1)S(1)} %get-tuple-element.5.decode_res), custom_call_target="tpu_custom_call" | custom-call | tf_op jit(solution)/shard_map/store/pallas_call | solution.py:430

commit v4 on v3

--- a/solution.py
+++ b/solution.py
@@ -204,8 +204,6 @@
                     acc[rows, left:right] = product
 
     def project_block(b, _):
-        wait(block_copies(b))
-
         @pl.when(b + LOOK < NH)
         def _():
             start(block_copies(b + LOOK))
@@ -218,6 +216,7 @@
         def _():
             pick()
 
+        wait(block_copies(b))
         at = pl.ds(pl.multiple_of(b * FEAT, FEAT), FEAT)
 
         @pl.when(b > SEND_BLOCK)

time: 30.8 us -> 30.8 us (level)
  no operation moved by 1% of the time
where the time goes in v4:
time: 30.8 us; the launch traced here: 30.6 us
  Pallas kernels  30 us (97%)
  between operations  0.64 us (2%)
    pallas_call x1, Pallas kernels, body(): pl.pallas_call(kernel, out_shape=(pltpu.VMEM((TOK, QW), bf16), pltpu.VMEM...  29 us
    pallas_call x1, Pallas kernels, body(): pl.pallas_call(store_kernel, out_shape=(jax.ShapeDtypeStruct((TOK, QW), b...  0.99 us

profile of v4, /device:TPU:0, one launch (start us, length us, event | category | flops | bytes accessed | tf_op | source)
XLA Modules:
  0.0 30.6 jit_solution(5800471322422024296)
XLA Ops:
  0.6 29.0 %layer.1 = (bf16[512,1024]{1,0:T(8,128)(2,1)S(1)}, bf16[8,4,1024]{2,1,0:T(4,128)(2,1)S(1)}) custom-call(bf16[512,8192]{1,0:T(8,128)(2,1)} %tokens.1, bf16[8192,1024]{1,0:T(8,128)(2,1)} %w_query.1, bf16[8192,128]{1,0:T(8,128)(2,1)} %w_key.1, bf16[8192,128]{1,0:T(8,128)(2,1)} %w_value.1, bf16[1024]{0:T(1024)(128)(2,1)} %b_query.1, bf16[128]{0:T(256)(128)(2,1)} %b_key.1, ...), custom_call_target="tpu_custom_call" | custom-call | tf_op jit(solution)/shard_map/layer/pallas_call | solution.py:371
  29.7 1.0 %store.1 = (bf16[512,1024]{1,0:T(8,128)(2,1)}, bf16[8,4,1024]{2,1,0:T(4,128)(2,1)}) custom-call(bf16[512,1024]{1,0:T(8,128)(2,1)S(1)} %get-tuple-element.4.prompt_res, bf16[8,4,1024]{2,1,0:T(4,128)(2,1)S(1)} %get-tuple-element.5.decode_res), custom_call_target="tpu_custom_call" | custom-call | tf_op jit(solution)/shard_map/store/pallas_call | solution.py:429
